TPU v7x, 512 devices: a whole 4x4x16 slice. The times are simulated.
512 devices in a mesh: param: 128 (over y_lo, x, z), freq: 4 (over y_hi, core).
Axes of the slice: x: 4, y: 4 (y_hi: 2, y_lo: 2; y = y_hi * 2 + y_lo), z: 16, core: 2. Of those that a mesh axis runs over, the one named last changes fastest.
Arguments:
- direction: bfloat16 [420, 8, 65536], P('freq', None, 'param'), may hold values from -6 to 6
- green_blocks: bfloat16 [8, 2, 600, 65536], P('freq', None, None, 'param'), may hold values from -0.0234375 to 0.0234375
- block_mask: int32 [8, 512], P(None, 'param'), may hold values 0 or 1
- noise_weights: float32 [8, 600], P('freq'), may hold values from 17 to 132
- prior_precision: float32 [65536], P('param'), may hold values from 0.05 to 0.5
- freq_index: int32 [8], replicated, may hold values from 1 to 209, as said below
Outputs:
- hessian_action: bfloat16 [420, 8, 65536], P('freq', None, 'param')
Inputs may be any that keep to these rules, and one draw needn't show every extreme that they name: `freq_index`: distinct values.
All inputs are finite; a program needn't handle non-finite values. No bound on the sum of `block_mask` on one device may be relied on, other than what follows from the above.
Results may differ from a plain program's by a relative error of at most 0.012.
Values may be sent and summed in bfloat16 or wider, within the bound.
A program may use at most 64 MiB of HBM per device.

v0:
```python
import math

import jax
import jax.numpy as jnp
from jax import lax
from jax.sharding import PartitionSpec as P

NT = 420
NF = 8
SBLK = 8
PBLK = 128


def tables(freq_index, times):
    phase = freq_index[:, None] * times[None, :] % NT
    angle = phase.astype(jnp.float32) * (2.0 * math.pi / NT)
    factor = 1.0 / math.sqrt(NT)
    return jnp.stack([jnp.cos(angle) * factor, -jnp.sin(angle) * factor], axis=1).astype(
        jnp.bfloat16
    )


def expand_mask(block_mask, sensors, columns):
    blocks = block_mask.astype(jnp.bfloat16)
    grid = jnp.broadcast_to(
        blocks[:, None, :, None], (SBLK, sensors // SBLK, blocks.shape[1], PBLK)
    )
    return grid.reshape(sensors, columns)


def contract(left, right):
    return jnp.einsum("wrp,wsp->wrs", left, right, preferred_element_type=jnp.float32)


def spread(left, right):
    return jnp.einsum("wrs,wsp->wrp", left, right, preferred_element_type=jnp.float32)


def on_device(direction, green_blocks, block_mask, noise_weights, prior_precision, freq_index):
    local_times, rhs_count, columns = direction.shape
    all_times = jnp.arange(NT, dtype=jnp.int32)
    own_times = lax.axis_index("freq") * local_times + jnp.arange(local_times, dtype=jnp.int32)
    table_all = tables(freq_index, all_times).reshape(2 * NF, NT)
    moved = lax.all_to_all(direction, "freq", split_axis=2, concat_axis=0, tiled=True)
    result = jnp.einsum("kt,trp->krp", table_all, moved, preferred_element_type=jnp.float32)
    spectra = result.reshape(NF, 2, moved.shape[1], moved.shape[2]).astype(jnp.bfloat16)
    spectrum = lax.all_to_all(spectra, "freq", split_axis=0, concat_axis=3, tiled=True)
    masks = expand_mask(block_mask, green_blocks.shape[2], columns)
    kernel = green_blocks * masks[None, None]
    kernel_real, kernel_imag = (kernel[:, 0], kernel[:, 1])
    spec_real, spec_imag = (spectrum[:, 0], spectrum[:, 1])
    data_real = contract(spec_real, kernel_real) - contract(spec_imag, kernel_imag)
    data_imag = contract(spec_real, kernel_imag) + contract(spec_imag, kernel_real)
    partial_data = jnp.stack([data_real, data_imag], axis=1)
    scaling = noise_weights[:, None, None, :]
    totals = lax.psum(partial_data, "param")
    weighted = (totals * scaling).astype(jnp.bfloat16)
    weighted_real, weighted_imag = (weighted[:, 0], weighted[:, 1])
    image_real = spread(weighted_real, kernel_real) + spread(weighted_imag, kernel_imag)
    image_imag = spread(weighted_imag, kernel_real) - spread(weighted_real, kernel_imag)
    image = jnp.stack([image_real, image_imag], axis=1).astype(jnp.bfloat16)
    damped = prior_precision[None, None, :] * direction
    table_back = 2 * tables(freq_index, own_times)
    summed = jnp.einsum(
        "wct,wcrp->trp",
        table_back,
        lax.all_gather(image, "freq", axis=0, tiled=True),
        preferred_element_type=jnp.float32,
    )
    return (damped + summed).astype(jnp.bfloat16)


def solution(mesh):
    placed = (
        P("freq", None, "param"),
        P("freq", None, None, "param"),
        P(None, "param"),
        P("freq", None),
        P("param"),
        P(),
    )
    return jax.shard_map(
        on_device, mesh=mesh, in_specs=placed, out_specs=P("freq", None, "param"), check_vma=False
    )
```

profile of v0, /device:TPU:1, one launch (start us, length us, event | category | flops | bytes accessed | tf_op | source)
XLA Modules:
  0.0 1085.6 jit_solution(5531064590202594670)
XLA Ops:
  6.5 2.8 copy.51
  9.4 10.5 all-to-all-start
  20.2 0.9 copy.76
  21.3 2.1 copy_multiply_fusion
  23.4 11.6 %all-to-all-done = bf16[105,8,512]{0,1,2:T(8,128)(2,1)S(1)} async-done(((bf16[105,8,512]{0,1,2:T(8,128)(2,1)}), bf16[105,8,512]{0,1,2:T(8,128)(2,1)S(1)}, u32[]{:S(2)}, u32[]{:S(2)}) %all-to-all-start) | async-done | bytes 860192 | tf_op jit(solution)/shard_map/all_to_all | solution.py:44
  35.0 1.8 copy.52
  36.8 1.3 copy.53
  38.4 0.6 copy.55
  39.0 4.1 all-to-all-start.1
  43.1 4.7 all-to-all-done.1
  47.8 0.4 fusion.12
  48.2 0.4 fusion.11
  48.6 0.4 fusion.1
  49.1 0.4 fusion.2
  49.5 0.7 pad_maximum_fusion
  50.3 973.5 %all-reduce.2.cloned.1.call-done = f32[2,2,8,600]{3,2,0,1:T(8,128)} async-done(((f32[2,2,8,600]{3,2,0,1:T(8,128)}), f32[2,2,8,600]{3,2,0,1:T(8,128)}) %all-reduce.2.cloned.1.call-update) | async-done | bytes 76816 | tf_op jit(solution)/shard_map/psum | solution.py:56
  1023.8 0.9 multiply_convert_fusion
  1024.7 0.3 fusion.9
  1025.0 0.3 fusion.10
  1025.3 0.3 fusion.5
  1025.5 0.3 fusion.6
  1025.8 50.5 %all_gather.3 = bf16[8,2,8,512]{3,2,0,1:T(8,128)(2,1)S(1)} all-gather(bf16[2,2,8,512]{3,2,0,1:T(8,128)(2,1)S(1)} %pad_maximum_fusion.1), channel_id=1, replica_groups=mesh['param'=128,'freq'=4] {'freq'}, dimensions={0}, use_global_device_ids=true | all-gather | bytes 163840 | tf_op jit(solution)/shard_map/all_gather | solution.py:67
  1076.3 0.4 convolution_bitcast_fusion
  1076.8 1.9 fusion
  (21 shorter events, 0.9 us)
Async XLA Ops:
  6.5 13.3 %copy-start.4 = (s32[8,4]{0,1:T(4,128)S(1)}, s32[8,4]{0,1:T(4,128)}, u32[]{:S(2)}) copy-start(s32[8,4]{0,1:T(4,128)} %param.8) | copy-start | bytes 388
  9.4 11.8 %copy-start.3 = (s32[8]{0:T(128)S(1)}, s32[8]{0:T(128)}, u32[]{:S(2)}) copy-start(s32[8]{0:T(128)} %param.11) | copy-start | bytes 100
  9.4 25.6 %all-to-all-start = ((bf16[105,8,512]{0,1,2:T(8,128)(2,1)}), bf16[105,8,512]{0,1,2:T(8,128)(2,1)S(1)}, u32[]{:S(2)}, u32[]{:S(2)}) async-start(bf16[105,8,512]{0,1,2:T(8,128)(2,1)} %copy.51), calls=%async_computation | async-start | bytes 2097152 | tf_op jit(solution)/shard_map/all_to_all | solution.py:44
  39.0 8.8 all-to-all-start.1
  43.1 980.7 %all-reduce.2.cloned.1.call-start = ((), (), s32[]{:S(2)}) async-start(), calls=%async_computation.2 | async-start | bytes 163840 | tf_op jit(solution)/shard_map/psum | solution.py:56
  48.2 975.6 %copy-start.1 = (f32[2,600]{1,0:T(2,128)S(1)}, f32[2,600]{1,0:T(2,128)}, u32[]{:S(2)}) copy-start(f32[2,600]{1,0:T(2,128)} %param.9) | copy-start | bytes 14404
  1025.5 51.3 %copy-start = (bf16[105,8,512]{2,1,0:T(8,128)(2,1)S(1)}, bf16[105,8,512]{2,1,0:T(8,128)(2,1)}, u32[]{:S(2)}) copy-start(bf16[105,8,512]{2,1,0:T(8,128)(2,1)} %param.6) | copy-start | bytes 2580484
  1025.5 51.3 %copy-start.2 = (f32[512]{0:T(512)S(1)}, f32[512]{0:T(512)}, u32[]{:S(2)}) copy-start(f32[512]{0:T(512)} %param.10) | copy-start | bytes 6148
Sparse Core Ops, SparseCore 0:
  50.3 973.4 all-reduce.1
where the time goes:
time: 1090 us
  waiting for transfers between devices  990 us (91%)
  blocking collectives  50.5 us (5%)
  starting transfers between devices  14.6 us (1%)
  between operations  13.4 us (1%)
    psum x1, waiting for transfers between devices, on_device(): totals = lax.psum(partial_data, 'param')  974 us
    all_gather x1, blocking collectives, on_device(): lax.all_gather(image, 'freq', axis=0, tiled=True)  50.5 us
  transfers between devices with their start and end apart: 3, of which 3 were waited for; matrix products, arithmetic and copies ran while one was open for 0% of the time, Pallas kernels for 0%

commit v1 on v0

v1 whole, which is shorter than its diff:
```python
import functools
import math

import jax
import jax.numpy as jnp
from jax import lax
from jax.experimental import pallas as pl
from jax.experimental.pallas import tpu as pltpu
from jax.sharding import PartitionSpec as P

NT = 420
NF = 8
RHS = 8
SENSORS = 600
SBLK = 8
PBLK = 128
LANES = 128
PLANE = 8
MESH = pl.DeviceIdType.MESH
F32 = jnp.float32
BF16 = jnp.bfloat16


def trig(freq, component, time):
    turn = freq * time + component * (NT // 4)
    phase = turn - NT * jnp.floor(turn * (1.0 / NT))
    phase = jnp.where(phase < 0, phase + NT, phase)
    phase = jnp.where(phase >= NT, phase - NT, phase)
    y = (jnp.abs(phase - NT // 2) - NT // 4) * (2.0 * math.pi / NT)
    s = y * y
    poly = -1.0 / 39916800
    for coef in (1.0 / 362880, -1.0 / 5040, 1.0 / 120, -1.0 / 6, 1.0):
        poly = poly * s + coef
    return poly * y * (1.0 / math.sqrt(NT))


def expanded_table(freq_ref, first_time, rows, columns, key_axis):
    key_shape = (rows, 1) if key_axis == 0 else (1, columns)
    step_shape = (1, columns) if key_axis == 0 else (rows, 1)
    key = lax.broadcasted_iota(jnp.int32, key_shape, key_axis)
    step = lax.broadcasted_iota(jnp.int32, step_shape, 1 - key_axis)
    freq = jnp.zeros(key_shape, F32)
    for w in range(NF):
        freq = jnp.where(key // (2 * RHS) == w, freq_ref[w].astype(F32), freq)
    component = (key // RHS % 2).astype(F32)
    time = (step // RHS + first_time).astype(F32)
    values = trig(freq, component, time)
    return jnp.where(key % RHS == step % RHS, values, 0.0)


def forward_kernel(
    ring, n_freq, dir_hbm, green_hbm, mask_ref, noise_ref, freq_ref,
    image_out, back_out,
    dirs, green, kern, mask, back, noise,
    spec_own, spec_send, spec_recv, data_send, data_recv, sum_send, sum_recv, weighted, image_send,
    load_sem, local_sem,
    spec_ssem, spec_rsem, data_ssem, data_rsem, sum_ssem, sum_rsem, w_ssem, w_rsem, im_ssem, im_rsem,
):
    param = lax.axis_index("param")
    q = lax.axis_index("freq")
    k, z = param // ring, param % ring
    times = dirs.shape[0]
    columns = dirs.shape[2]
    own_w = NF // n_freq
    rows = own_w * 2 * RHS
    tiles = data_send.shape[0]
    padded = tiles * LANES

    def freq_peer(off):
        return (param, (q + off) % n_freq)

    def plane_peer(to):
        return (to * ring + z, q)

    def ring_peer(off):
        return (k * ring + (z + off) % ring, q)

    def remote(src, dst, ssem, rsem, to):
        return pltpu.make_async_remote_copy(
            src_ref=src, dst_ref=dst, send_sem=ssem, recv_sem=rsem, device_id=to, device_id_type=MESH
        )

    load_dir = pltpu.make_async_copy(dir_hbm, dirs, load_sem.at[0])
    load_dir.start()
    load_green = pltpu.make_async_copy(green_hbm, green, load_sem.at[1])
    load_green.start()

    barrier = pltpu.get_barrier_semaphore()
    peers = [freq_peer(o) for o in range(1, n_freq)]
    peers += [plane_peer((k + o) % PLANE) for o in range(1, PLANE)]
    peers += [ring_peer(o) for o in range(1, ring)]
    for peer in peers:
        pl.semaphore_signal(barrier, inc=1, device_id=peer, device_id_type=MESH)

    table = expanded_table(freq_ref, q * times, NF * 2 * RHS, times * RHS, 0).astype(BF16)
    load_dir.wait()
    steps = dirs[...].astype(F32).reshape(times * RHS, columns).astype(BF16)
    part = jnp.dot(table, steps, preferred_element_type=F32)
    for g in range(n_freq):
        piece = part[g * rows : (g + 1) * rows]
        spec_own[g] = piece
        spec_send[g] = piece.astype(BF16)

    pl.semaphore_wait(barrier, len(peers))
    spec_copies = []
    for off in range(1, n_freq):
        copy = remote(
            spec_send.at[(q + off) % n_freq], spec_recv.at[off - 1], spec_ssem.at[off - 1], spec_rsem.at[off - 1],
            freq_peer(off),
        )
        copy.start()
        spec_copies.append(copy)

    sensor = lax.broadcasted_iota(jnp.int32, (padded, SBLK), 0)
    block = lax.broadcasted_iota(jnp.int32, (padded, SBLK), 1)
    per = SENSORS // SBLK
    picks = jnp.where((sensor >= block * per) & (sensor < (block + 1) * per), 1.0, 0.0).astype(BF16)
    block8 = lax.broadcasted_iota(jnp.int32, (SBLK, LANES), 0)
    parts = []
    for b in range(columns // PBLK):
        value = jnp.zeros((SBLK, LANES), F32)
        for s in range(SBLK):
            value = jnp.where(block8 == s, mask_ref[b, s].astype(F32), value)
        parts.append(value)
    blocks = jnp.concatenate(parts, axis=1).astype(BF16)
    mask[...] = jnp.dot(picks, blocks, preferred_element_type=F32).astype(BF16)
    load_green.wait()
    for w in range(own_w):
        for c in range(2):
            kern[w, c, :SENSORS, :] = green[w, c] * mask[:SENSORS, :]
            kern[w, c, SENSORS:, :] = jnp.zeros((padded - SENSORS, columns), BF16)
    noise[...] = jnp.zeros_like(noise)
    for j in range(tiles):
        width = min(LANES, SENSORS - j * LANES)
        noise[j, :, :width] = noise_ref[:, j * LANES : j * LANES + width]

    total = spec_own[q]
    for off, copy in enumerate(spec_copies):
        copy.wait_recv()
        total = total + spec_recv[off].astype(F32)

    for w in range(own_w):
        first = total[w * 2 * RHS : (w + 1) * 2 * RHS]
        second = jnp.concatenate([-first[RHS:], first[:RHS]], axis=0)
        data = lax.dot_general(
            first.astype(BF16), kern[w, 0], (((1,), (1,)), ((), ())), preferred_element_type=F32
        ) + lax.dot_general(
            second.astype(BF16), kern[w, 1], (((1,), (1,)), ((), ())), preferred_element_type=F32
        )
        data = data.astype(BF16)
        for j in range(tiles):
            data_send[j, w * 2 * RHS : (w + 1) * 2 * RHS, :] = data[:, j * LANES : (j + 1) * LANES]

    def data_copy(off):
        to = (k + off) % PLANE
        return to, remote(
            data_send.at[to % tiles], data_recv.at[off - 1], data_ssem.at[off - 1], data_rsem.at[off - 1], plane_peer(to)
        )

    def sum_copy(off):
        return remote(sum_send, sum_recv.at[off - 1], sum_ssem.at[off - 1], sum_rsem.at[off - 1], ring_peer(off))

    def weighted_copy(off):
        own = k % tiles
        return remote(
            weighted.at[own], weighted.at[own], w_ssem.at[off - 1], w_rsem.at[own], plane_peer((k + off) % PLANE)
        )

    for off in range(1, PLANE):
        to, copy = data_copy(off)
        pl.when(to < tiles)(copy.start)

    back[...] = (
        (2.0 * expanded_table(freq_ref, q * times, times * RHS, NF * 2 * RHS, 1))
        .reshape(times, RHS, NF * 2 * RHS)
        .astype(BF16)
    )
    store_back = pltpu.make_async_copy(back, back_out, local_sem.at[0])
    store_back.start()

    @pl.when(k < tiles)
    def _():
        own = k % tiles
        acc = data_send[own].astype(F32)
        for off in range(1, PLANE):
            data_copy(off)[1].wait_recv()
            acc = acc + data_recv[off - 1].astype(F32)
        sum_send[...] = acc.astype(BF16)
        for off in range(1, ring):
            sum_copy(off).start()
        for off in range(1, ring):
            sum_copy(off).wait_recv()
            acc = acc + sum_recv[off - 1].astype(F32)
        scale = noise[own]
        scaled = [acc[w * 2 * RHS : (w + 1) * 2 * RHS] * scale[w : w + 1] for w in range(own_w)]
        weighted[own] = jnp.concatenate(scaled, axis=0).astype(BF16)
        for off in range(1, PLANE):
            weighted_copy(off).start()

    for j in range(tiles):
        arrival = remote(weighted.at[j], weighted.at[j], w_ssem.at[0], w_rsem.at[j], plane_peer((k + 1) % PLANE))
        pl.when(k != j)(arrival.wait_recv)

    for w in range(own_w):
        here = slice(w * 2 * RHS, (w + 1) * 2 * RHS)
        first = jnp.concatenate([weighted[j, here, :] for j in range(tiles)], axis=1)
        wide = first.astype(F32)
        second = jnp.concatenate([wide[RHS:], -wide[:RHS]], axis=0).astype(BF16)
        image = jnp.dot(first, kern[w, 0], preferred_element_type=F32) + jnp.dot(
            second, kern[w, 1], preferred_element_type=F32
        )
        image_send[here, :] = image.astype(BF16)

    image_copies = []
    for off in range(1, n_freq):
        copy = remote(image_send, image_out.at[q], im_ssem.at[off - 1], im_rsem.at[off - 1], freq_peer(off))
        copy.start()
        image_copies.append(copy)
    keep = pltpu.make_async_copy(image_send, image_out.at[q], local_sem.at[1])
    keep.start()

    for copy in spec_copies:
        copy.wait_send()
    for off in range(1, PLANE):
        to, copy = data_copy(off)
        pl.when(to < tiles)(copy.wait_send)

    @pl.when(k < tiles)
    def _():
        for off in range(1, ring):
            sum_copy(off).wait_send()
        for off in range(1, PLANE):
            weighted_copy(off).wait_send()

    store_back.wait()
    keep.wait()
    for copy in image_copies:
        copy.wait()


def back_kernel(table_ref, image_ref, prior_ref, dir_ref, out_ref):
    times, _, keys = table_ref.shape
    columns = dir_ref.shape[2]
    table = table_ref[...].astype(F32).reshape(times * RHS, keys).astype(BF16)
    summed = jnp.dot(table, image_ref[...], preferred_element_type=F32)
    damped = dir_ref[...].astype(F32).reshape(times * RHS, columns) * prior_ref[...]
    out_ref[...] = (summed + damped).reshape(times, RHS, columns).astype(BF16)


def on_device(ring, n_freq, direction, green_blocks, block_mask, noise_weights, prior_precision, freq_index):
    times, _, columns = direction.shape
    own_w = NF // n_freq
    rows = own_w * 2 * RHS
    keys = NF * 2 * RHS
    tiles = -(-SENSORS // LANES)
    padded = tiles * LANES
    vmem = pltpu.VMEM
    dma = pltpu.SemaphoreType.DMA
    anywhere = pl.BlockSpec(memory_space=pl.ANY)
    images, back = pl.pallas_call(
        functools.partial(forward_kernel, ring, n_freq),
        out_shape=(
            jax.ShapeDtypeStruct((n_freq, rows, columns), BF16),
            jax.ShapeDtypeStruct((times, RHS, keys), BF16),
        ),
        in_specs=[
            anywhere,
            anywhere,
            pl.BlockSpec(memory_space=pltpu.SMEM),
            pl.BlockSpec(memory_space=pltpu.VMEM),
            pl.BlockSpec(memory_space=pltpu.SMEM),
        ],
        out_specs=(anywhere, anywhere),
        scratch_shapes=[
            vmem((times, RHS, columns), BF16),
            vmem((own_w, 2, SENSORS, columns), BF16),
            vmem((own_w, 2, padded, columns), BF16),
            vmem((padded, columns), BF16),
            vmem((times, RHS, keys), BF16),
            vmem((tiles, own_w, LANES), F32),
            vmem((n_freq, rows, columns), F32),
            vmem((n_freq, rows, columns), BF16),
            vmem((n_freq - 1, rows, columns), BF16),
            vmem((tiles, rows, LANES), BF16),
            vmem((PLANE - 1, rows, LANES), BF16),
            vmem((rows, LANES), BF16),
            vmem((ring - 1, rows, LANES), BF16),
            vmem((tiles, rows, LANES), BF16),
            vmem((rows, columns), BF16),
            dma((2,)),
            dma((2,)),
            dma((n_freq - 1,)),
            dma((n_freq - 1,)),
            dma((PLANE - 1,)),
            dma((PLANE - 1,)),
            dma((ring - 1,)),
            dma((ring - 1,)),
            dma((PLANE - 1,)),
            dma((tiles,)),
            dma((n_freq - 1,)),
            dma((n_freq - 1,)),
        ],
        compiler_params=pltpu.CompilerParams(
            collective_id=0, has_side_effects=True, vmem_limit_bytes=32 * 1024 * 1024
        ),
        name="forward",
    )(direction, green_blocks, block_mask.T, noise_weights, freq_index)

    chunk = times // 3
    return pl.pallas_call(
        back_kernel,
        grid=(times // chunk,),
        out_shape=jax.ShapeDtypeStruct(direction.shape, BF16),
        in_specs=[
            pl.BlockSpec((chunk, RHS, keys), lambda i: (i, 0, 0)),
            pl.BlockSpec((keys, columns), lambda i: (0, 0)),
            pl.BlockSpec((1, columns), lambda i: (0, 0)),
            pl.BlockSpec((chunk, RHS, columns), lambda i: (i, 0, 0)),
        ],
        out_specs=pl.BlockSpec((chunk, RHS, columns), lambda i: (i, 0, 0)),
        compiler_params=pltpu.CompilerParams(vmem_limit_bytes=16 * 1024 * 1024),
        name="backward",
    )(back, images.reshape(keys, columns), prior_precision.reshape(1, columns), direction)


def solution(mesh):
    n_freq = mesh.shape["freq"]
    ring = mesh.shape["param"] // PLANE
    placed = (
        P("freq", None, "param"),
        P("freq", None, None, "param"),
        P(None, "param"),
        P("freq", None),
        P("param"),
        P(),
    )
    return jax.shard_map(
        functools.partial(on_device, ring, n_freq),
        mesh=mesh,
        in_specs=placed,
        out_specs=P("freq", None, "param"),
        check_vma=False,
    )
```

time: 1090 us -> 50.2 us (0.05)
  waiting for transfers between devices: 990 us -> 0 us
  blocking collectives: 50.5 us -> 0 us
  Pallas kernels: 0 us -> 45 us
  starting transfers between devices: 14.6 us -> 0 us
  between operations: 13.4 us -> 0.02 us
    psum x1 -> x0, waiting for transfers between devices: 974 us -> none  [on_device(): totals = lax.psum(partial_data, 'param')]
    all_gather x1 -> x0, blocking collectives: 50.5 us -> none  [on_device(): lax.all_gather(image, 'freq', axis=0, tiled=True)]
    pallas_call x0 -> x2, Pallas kernels: none -> 45 us  [the longest x1 43.1 us: on_device(): pl.pallas_call(functools.partial(forward_kernel, ring, n_freq), out_shape...]
    all_to_all x2 -> x0, waiting for transfers between devices: 16.3 us -> none  [the longest x1 11.6 us: on_device(): lax.all_to_all(direction, 'freq', split_axis=2, concat_axis=0, tiled=True)]
    all_to_all x2 -> x0, starting transfers between devices: 14.6 us -> none  [the longest x1 10.5 us: on_device(): lax.all_to_all(direction, 'freq', split_axis=2, concat_axis=0, tiled=True)]
  transfers between devices with their start and end apart: 3 -> 0, of which waited for: 3 -> 0; matrix products, arithmetic and copies ran while one was open for 0% -> 0% of each run, Pallas kernels for 0% -> 0%
where the time goes in v1:
time: 50.2 us; the launch traced here: 49.9 us
  Pallas kernels  45 us (90%)
  local copies, waits for them, and re-layouts  4.89 us (10%)
    pallas_call x1, Pallas kernels, on_device(): pl.pallas_call(functools.partial(forward_kernel, ring, n_freq), out_shape...  43.1 us
    unnamed x12, local copies, waits for them, and re-layouts  4.89 us
    pallas_call x1, Pallas kernels, on_device(): pl.pallas_call(back_kernel, grid=(times // chunk,), out_shape=jax.ShapeDt...  1.89 us

profile of v1, /device:TPU:1, one launch (start us, length us, event | category | flops | bytes accessed | tf_op | source)
XLA Modules:
  0.0 49.9 jit_solution(18300162627658695443)
XLA Ops:
  0.0 0.0 copy-start.4
  0.0 0.0 copy-start
  0.0 1.2 %copy-done = bf16[105,8,512]{2,1,0:T(8,128)(2,1)S(1)} copy-done((bf16[105,8,512]{2,1,0:T(8,128)(2,1)S(1)}, bf16[105,8,512]{2,1,0:T(8,128)(2,1)}, u32[]{:S(2)}) %copy-start) | copy-done | bytes 860184
  1.2 0.0 copy-start.1
  1.2 1.7 %copy-done.1 = bf16[2,2,600,512]{3,2,1,0:T(8,128)(2,1)S(1)} copy-done((bf16[2,2,600,512]{3,2,1,0:T(8,128)(2,1)S(1)}, bf16[2,2,600,512]{3,2,1,0:T(8,128)(2,1)}, u32[]{:S(2)}) %copy-start.1) | copy-done | bytes 2457624
  2.9 0.0 copy-start.2
  2.9 0.7 %copy-done.2 = f32[2,600]{1,0:T(2,128)S(1)} copy-done((f32[2,600]{1,0:T(2,128)S(1)}, f32[2,600]{1,0:T(2,128)}, u32[]{:S(2)}) %copy-start.2) | copy-done | bytes 4824
  3.6 0.0 copy-start.3
  3.6 0.7 %copy-done.3 = s32[8,4]{0,1:T(4,128)S(1)} copy-done((s32[8,4]{0,1:T(4,128)S(1)}, s32[8,4]{0,1:T(4,128)}, u32[]{:S(2)}) %copy-start.3) | copy-done | bytes 152
  4.2 0.0 copy-start.5
  4.2 0.7 %copy-done.5 = s32[8]{0:T(128)S(1)} copy-done((s32[8]{0:T(128)S(1)}, s32[8]{0:T(128)}, u32[]{:S(2)}) %copy-start.5) | copy-done | bytes 56
  4.9 43.1 %forward.1 = (bf16[4,32,512]{2,1,0:T(8,128)(2,1)S(1)}, bf16[105,8,128]{2,1,0:T(8,128)(2,1)S(1)}) custom-call(bf16[105,8,512]{2,1,0:T(8,128)(2,1)S(1)} %copy-done, bf16[2,2,600,512]{3,2,1,0:T(8,128)(2,1)S(1)} %copy-done.1, s32[4,8]{1,0:T(4,128)S(1)} %bitcast.4, f32[2,600]{1,0:T(2,128)S(1)} %copy-done.2, s32[8]{0:T(128)S(1)} %copy-done.5), custom_call_target="tpu_custom_call" | custom-call | tf_op jit(solution)/shard_map/forward/pallas_call | solution.py:260
  48.0 0.0 copy-done.4
  48.0 1.9 %backward.1 = bf16[105,8,512]{2,1,0:T(8,128)(2,1)} custom-call(bf16[105,8,128]{2,1,0:T(8,128)(2,1)S(1)} %get-tuple-element.7.table_ref, bf16[128,512]{1,0:T(8,128)(2,1)S(1)} %bitcast.3, f32[1,512]{1,0:T(1,128)S(1)} %bitcast.5, bf16[105,8,512]{2,1,0:T(8,128)(2,1)S(1)} %copy-done), custom_call_target="tpu_custom_call" | custom-call | tf_op jit(solution)/shard_map/backward/pallas_call | solution.py:310
Async XLA Ops:
  0.0 48.0 %copy-start.4 = (f32[512]{0:T(512)S(1)}, f32[512]{0:T(512)}, u32[]{:S(2)}) copy-start(f32[512]{0:T(512)} %param.10) | copy-start | bytes 6148
  0.0 1.2 %copy-start = (bf16[105,8,512]{2,1,0:T(8,128)(2,1)S(1)}, bf16[105,8,512]{2,1,0:T(8,128)(2,1)}, u32[]{:S(2)}) copy-start(bf16[105,8,512]{2,1,0:T(8,128)(2,1)} %dir_ref.1) | copy-start | bytes 2580484
  1.2 1.7 %copy-start.1 = (bf16[2,2,600,512]{3,2,1,0:T(8,128)(2,1)S(1)}, bf16[2,2,600,512]{3,2,1,0:T(8,128)(2,1)}, u32[]{:S(2)}) copy-start(bf16[2,2,600,512]{3,2,1,0:T(8,128)(2,1)} %green_hbm.1) | copy-start | bytes 7372804
  2.9 0.7 %copy-start.2 = (f32[2,600]{1,0:T(2,128)S(1)}, f32[2,600]{1,0:T(2,128)}, u32[]{:S(2)}) copy-start(f32[2,600]{1,0:T(2,128)} %noise_ref.1) | copy-start | bytes 14404
  3.6 0.7 %copy-start.3 = (s32[8,4]{0,1:T(4,128)S(1)}, s32[8,4]{0,1:T(4,128)}, u32[]{:S(2)}) copy-start(s32[8,4]{0,1:T(4,128)} %param.8) | copy-start | bytes 388
  4.2 0.7 %copy-start.5 = (s32[8]{0:T(128)S(1)}, s32[8]{0:T(128)}, u32[]{:S(2)}) copy-start(s32[8]{0:T(128)} %freq_ref.1) | copy-start | bytes 100

commit v2 on v1

v2 whole, which is shorter than its diff:
```python
import functools
import math

import jax
import jax.numpy as jnp
from jax import lax
from jax.experimental import pallas as pl
from jax.experimental.pallas import tpu as pltpu
from jax.sharding import PartitionSpec as P

NT = 420
NF = 8
RHS = 8
SENSORS = 600
SBLK = 8
PBLK = 128
LANES = 128
PLANE = 8
MESH = pl.DeviceIdType.MESH
F32 = jnp.float32
BF16 = jnp.bfloat16


def trig(freq, component, time):
    turn = freq * time + component * (NT // 4)
    phase = turn - NT * jnp.floor(turn * (1.0 / NT))
    phase = jnp.where(phase < 0, phase + NT, phase)
    phase = jnp.where(phase >= NT, phase - NT, phase)
    y = (jnp.abs(phase - NT // 2) - NT // 4) * (2.0 * math.pi / NT)
    s = y * y
    poly = -1.0 / 39916800
    for coef in (1.0 / 362880, -1.0 / 5040, 1.0 / 120, -1.0 / 6, 1.0):
        poly = poly * s + coef
    return poly * y * (1.0 / math.sqrt(NT))


def expanded_table(freq_ref, first_time, rows, columns, key_axis):
    key_shape = (rows, 1) if key_axis == 0 else (1, columns)
    step_shape = (1, columns) if key_axis == 0 else (rows, 1)
    key = lax.broadcasted_iota(jnp.int32, key_shape, key_axis)
    step = lax.broadcasted_iota(jnp.int32, step_shape, 1 - key_axis)
    freq = jnp.zeros(key_shape, F32)
    for w in range(NF):
        freq = jnp.where(key // (2 * RHS) == w, freq_ref[w].astype(F32), freq)
    component = (key // RHS % 2).astype(F32)
    time = (step // RHS + first_time).astype(F32)
    values = trig(freq, component, time)
    return jnp.where(key % RHS == step % RHS, values, 0.0)


def forward_kernel(
    ring, n_freq, dir_hbm, green_hbm, mask_hbm, noise_hbm, freq_hbm,
    image_out,
    dirs, green, mask_ref, noise_ref, freq_ref, kern, mask, noise,
    spec_own, spec_send, spec_recv, data_send, data_recv, sum_own, sum_send, sum_recv, weighted, image_send,
    load_sem, local_sem, near_sem,
    spec_ssem, spec_rsem, data_ssem, data_rsem, more_ssem, more_rsem, sum_ssem, sum_rsem, w_ssem, w_rsem, im_ssem, im_rsem,
):
    param = lax.axis_index("param")
    q = lax.axis_index("freq")
    k, z = param // ring, param % ring
    core = q % 2
    times = dirs.shape[0]
    columns = dirs.shape[2]
    own_w = NF // n_freq
    pair = 2 * RHS
    rows = own_w * pair
    units = data_send.shape[0]
    tiles = units // own_w
    padded = tiles * LANES
    extra = units - PLANE
    has_extra = k // extra == core
    second_unit = PLANE + k % extra

    def freq_peer(off):
        return (param, (q + off) % n_freq)

    def plane_peer(to):
        return (to * ring + z, q)

    def ring_peer(off):
        return (k * ring + (z + off) % ring, q)

    def remote(src, dst, ssem, rsem, to):
        return pltpu.make_async_remote_copy(
            src_ref=src, dst_ref=dst, send_sem=ssem, recv_sem=rsem, device_id=to, device_id_type=MESH
        )

    def signal(semaphore, to):
        pl.semaphore_signal(semaphore, inc=1, device_id=to, device_id_type=MESH)

    load_freq, load_dir, load_mask, load_noise, load_green = [
        pltpu.make_async_copy(src, dst, load_sem.at[i])
        for i, (src, dst) in enumerate(
            ((freq_hbm, freq_ref), (dir_hbm, dirs), (mask_hbm, mask_ref), (noise_hbm, noise_ref), (green_hbm, green))
        )
    ]
    for load in (load_freq, load_dir, load_mask, load_noise, load_green):
        load.start()

    barrier = pltpu.get_barrier_semaphore()
    peers = [plane_peer((k + o) % PLANE) for o in range(1, PLANE)]
    peers += [freq_peer(o) for o in range(1, n_freq)]
    peers += [ring_peer(1), ring_peer(ring - 1)]
    for peer in peers:
        signal(barrier, peer)
    reaches = [d for d in (1, 2, 4, 8, 16) if 2 * d <= ring // 2]

    def reach_signal(i):
        signal(near_sem.at[i], ring_peer(reaches[i]))
        signal(near_sem.at[i], ring_peer(ring - reaches[i]))

    load_freq.wait()
    table = expanded_table(freq_ref, q * times, NF * pair, times * RHS, 0).astype(BF16)
    load_dir.wait()
    steps = dirs[...].astype(F32).reshape(times * RHS, columns).astype(BF16)
    part = jnp.dot(table, steps, preferred_element_type=F32)
    for g in range(n_freq):
        piece = part[g * rows : (g + 1) * rows]
        spec_own[g] = piece
        spec_send[g] = piece.astype(BF16)

    pl.semaphore_wait(barrier, len(peers))
    spec_copies = []
    for off in (2, 3, 1) if n_freq == 4 else range(1, n_freq):
        copy = remote(
            spec_send.at[(q + off) % n_freq], spec_recv.at[off - 1], spec_ssem.at[off - 1], spec_rsem.at[off - 1],
            freq_peer(off),
        )
        copy.start()
        spec_copies.append(copy)
    if reaches:
        reach_signal(0)

    load_mask.wait()
    sensor = lax.broadcasted_iota(jnp.int32, (padded, SBLK), 0)
    block = lax.broadcasted_iota(jnp.int32, (padded, SBLK), 1)
    per = SENSORS // SBLK
    picks = jnp.where((sensor >= block * per) & (sensor < (block + 1) * per), 1.0, 0.0).astype(BF16)
    block8 = lax.broadcasted_iota(jnp.int32, (SBLK, LANES), 0)
    parts = []
    for b in range(columns // PBLK):
        value = jnp.zeros((SBLK, LANES), F32)
        for s in range(SBLK):
            value = jnp.where(block8 == s, mask_ref[b, s].astype(F32), value)
        parts.append(value)
    blocks = jnp.concatenate(parts, axis=1).astype(BF16)
    mask[...] = jnp.dot(picks, blocks, preferred_element_type=F32).astype(BF16)
    load_green.wait()
    for w in range(own_w):
        for c in range(2):
            kern[w, c, :SENSORS, :] = green[w, c] * mask[:SENSORS, :]
            kern[w, c, SENSORS:, :] = jnp.zeros((padded - SENSORS, columns), BF16)
    if reaches:
        pl.semaphore_wait(near_sem.at[0], 2)
    if len(reaches) > 1:
        reach_signal(1)
    load_noise.wait()
    noise[...] = jnp.zeros_like(noise)
    for u in range(units):
        w, j = u // tiles, u % tiles
        width = min(LANES, SENSORS - j * LANES)
        noise[u, :, :width] = jnp.broadcast_to(noise_ref[w : w + 1, j * LANES : j * LANES + width], (pair, width))

    total = spec_own[q]
    for off, copy in zip((2, 3, 1) if n_freq == 4 else range(1, n_freq), spec_copies):
        copy.wait_recv()
        total = total + spec_recv[off - 1].astype(F32)

    for w in range(own_w):
        first = total[w * pair : (w + 1) * pair]
        second = jnp.concatenate([-first[RHS:], first[:RHS]], axis=0)
        data = lax.dot_general(
            first.astype(BF16), kern[w, 0], (((1,), (1,)), ((), ())), preferred_element_type=F32
        ) + lax.dot_general(
            second.astype(BF16), kern[w, 1], (((1,), (1,)), ((), ())), preferred_element_type=F32
        )
        data = data.astype(BF16)
        for j in range(tiles):
            data_send[w * tiles + j] = data[:, j * LANES : (j + 1) * LANES]

    def data_copy(off):
        to = (k + off) % PLANE
        return remote(data_send.at[to], data_recv.at[off, 0], data_ssem.at[off], data_rsem.at[off], plane_peer(to))

    def more_copy(j):
        to = extra * core + j
        off = (to - k + PLANE) % PLANE
        return to, remote(
            data_send.at[PLANE + j], data_recv.at[off, 1], more_ssem.at[j], more_rsem.at[off], plane_peer(to)
        )

    def more_arrival(off):
        return remote(
            data_send.at[0], data_recv.at[off, 1], more_ssem.at[0], more_rsem.at[off], plane_peer((k + off) % PLANE)
        )

    def sum_copy(off, count):
        here = pl.ds(0, count)
        return remote(sum_send.at[here], sum_recv.at[off, here], sum_ssem.at[off], sum_rsem.at[off], ring_peer(off))

    def weighted_copy(off, n, unit):
        return remote(
            weighted.at[unit], weighted.at[unit], w_ssem.at[n, off], w_rsem.at[unit], plane_peer((k + off) % PLANE)
        )

    far_plane = [off for off in (6, 2, 5, 7, 3, 1, 4)]
    far_ring = sorted(range(1, ring), key=lambda off: -min(off, ring - off))

    for j in range(extra):
        to, copy = more_copy(j)
        pl.when(k != to)(copy.start)
    for off in far_plane:
        data_copy(off).start()
    if len(reaches) > 1:
        pl.semaphore_wait(near_sem.at[1], 2)
    if len(reaches) > 2:
        reach_signal(2)

    acc = data_send[k].astype(F32)
    for off in reversed(far_plane):
        data_copy(off).wait_recv()
        acc = acc + data_recv[off, 0].astype(F32)
    sum_own[0] = acc
    sum_send[0] = acc.astype(BF16)
    if len(reaches) > 2:
        pl.semaphore_wait(near_sem.at[2], 2)

    @pl.when(has_extra)
    def _():
        acc = data_send[second_unit].astype(F32)
        for off in reversed(far_plane):
            more_arrival(off).wait_recv()
            acc = acc + data_recv[off, 1].astype(F32)
        sum_own[1] = acc
        sum_send[1] = acc.astype(BF16)
        for off in far_ring:
            sum_copy(off, 2).start()
        acc = sum_own[...]
        for off in reversed(far_ring):
            sum_copy(off, 2).wait_recv()
            acc = acc + sum_recv[off].astype(F32)
        weighted[k] = (acc[0] * noise[k]).astype(BF16)
        weighted[second_unit] = (acc[1] * noise[second_unit]).astype(BF16)
        for off in far_plane:
            weighted_copy(off, 0, k).start()
            weighted_copy(off, 1, second_unit).start()

    @pl.when(jnp.logical_not(has_extra))
    def _():
        for off in far_ring:
            sum_copy(off, 1).start()
        acc = sum_own[0]
        for off in reversed(far_ring):
            sum_copy(off, 1).wait_recv()
            acc = acc + sum_recv[off, 0].astype(F32)
        weighted[k] = (acc * noise[k]).astype(BF16)
        for off in far_plane:
            weighted_copy(off, 0, k).start()

    for u in range(units):
        owner = u if u < PLANE else extra * core + u - PLANE
        arrival = remote(weighted.at[u], weighted.at[u], w_ssem.at[0, 0], w_rsem.at[u], plane_peer((k + 1) % PLANE))
        pl.when(k != owner)(arrival.wait_recv)

    for w in range(own_w):
        here = slice(w * pair, (w + 1) * pair)
        first = jnp.concatenate([weighted[w * tiles + j] for j in range(tiles)], axis=1)
        wide = first.astype(F32)
        second = jnp.concatenate([wide[RHS:], -wide[:RHS]], axis=0).astype(BF16)
        image = jnp.dot(first, kern[w, 0], preferred_element_type=F32) + jnp.dot(
            second, kern[w, 1], preferred_element_type=F32
        )
        image_send[here, :] = image.astype(BF16)

    image_copies = []
    for off in (2, 3, 1) if n_freq == 4 else range(1, n_freq):
        copy = remote(image_send, image_out.at[q], im_ssem.at[off - 1], im_rsem.at[off - 1], freq_peer(off))
        copy.start()
        image_copies.append(copy)
    keep = pltpu.make_async_copy(image_send, image_out.at[q], local_sem.at[0])
    keep.start()

    for copy in spec_copies:
        copy.wait_send()
    for j in range(extra):
        to, copy = more_copy(j)
        pl.when(k != to)(copy.wait_send)
    for off in far_plane:
        data_copy(off).wait_send()
        weighted_copy(off, 0, k).wait_send()

    @pl.when(has_extra)
    def _():
        for off in far_ring:
            sum_copy(off, 2).wait_send()
        for off in far_plane:
            weighted_copy(off, 1, second_unit).wait_send()

    @pl.when(jnp.logical_not(has_extra))
    def _():
        for off in far_ring:
            sum_copy(off, 1).wait_send()

    keep.wait()
    for copy in image_copies:
        copy.wait()


def back_kernel(
    image_hbm, prior_hbm, dir_hbm, freq_hbm, out_hbm, image, prior, dirs, outs, freq_ref, load_sem, dir_sem, out_sem
):
    times, _, columns = dirs.shape
    chunks = dir_sem.shape[0]
    size = times // chunks
    keys = image.shape[0]
    first_time = lax.axis_index("freq") * times
    load_freq = pltpu.make_async_copy(freq_hbm, freq_ref, load_sem.at[0])
    load_image = pltpu.make_async_copy(image_hbm, image, load_sem.at[1])
    load_prior = pltpu.make_async_copy(prior_hbm, prior, load_sem.at[2])
    loads, stores = [], []
    for i in range(chunks):
        here = pl.ds(i * size, size)
        loads.append(pltpu.make_async_copy(dir_hbm.at[here], dirs.at[here], dir_sem.at[i]))
        stores.append(pltpu.make_async_copy(outs.at[here], out_hbm.at[here], out_sem.at[i]))
    for load in [load_freq, load_image, load_prior] + loads:
        load.start()
    load_freq.wait()
    tables = [
        (2.0 * expanded_table(freq_ref, first_time + i * size, size * RHS, keys, 1)).astype(BF16) for i in range(chunks)
    ]
    load_prior.wait()
    load_image.wait()
    for i in range(chunks):
        here = slice(i * size, (i + 1) * size)
        summed = jnp.dot(tables[i], image[...], preferred_element_type=F32)
        loads[i].wait()
        damped = dirs[here].astype(F32).reshape(size * RHS, columns) * prior[...]
        outs[here] = (summed + damped).reshape(size, RHS, columns).astype(BF16)
        stores[i].start()
    for store in stores:
        store.wait()


def on_device(ring, n_freq, direction, green_blocks, block_mask, noise_weights, prior_precision, freq_index):
    times, _, columns = direction.shape
    own_w = NF // n_freq
    pair = 2 * RHS
    rows = own_w * pair
    keys = NF * pair
    tiles = -(-SENSORS // LANES)
    units = own_w * tiles
    padded = tiles * LANES
    vmem = pltpu.VMEM
    dma = pltpu.SemaphoreType.DMA
    anywhere = pl.BlockSpec(memory_space=pl.ANY)
    images = pl.pallas_call(
        functools.partial(forward_kernel, ring, n_freq),
        out_shape=jax.ShapeDtypeStruct((n_freq, rows, columns), BF16),
        in_specs=[anywhere] * 5,
        out_specs=anywhere,
        scratch_shapes=[
            vmem((times, RHS, columns), BF16),
            vmem((own_w, 2, SENSORS, columns), BF16),
            pltpu.SMEM(block_mask.shape[::-1], jnp.int32),
            vmem((own_w, SENSORS), F32),
            pltpu.SMEM((NF,), jnp.int32),
            vmem((own_w, 2, padded, columns), BF16),
            vmem((padded, columns), BF16),
            vmem((units, pair, LANES), F32),
            vmem((n_freq, rows, columns), F32),
            vmem((n_freq, rows, columns), BF16),
            vmem((n_freq - 1, rows, columns), BF16),
            vmem((units, pair, LANES), BF16),
            vmem((PLANE, 2, pair, LANES), BF16),
            vmem((2, pair, LANES), F32),
            vmem((2, pair, LANES), BF16),
            vmem((ring, 2, pair, LANES), BF16),
            vmem((units, pair, LANES), BF16),
            vmem((rows, columns), BF16),
            dma((5,)),
            dma((1,)),
            pltpu.SemaphoreType.REGULAR((4,)),
            dma((n_freq - 1,)),
            dma((n_freq - 1,)),
            dma((PLANE,)),
            dma((PLANE,)),
            dma((2,)),
            dma((PLANE,)),
            dma((ring,)),
            dma((ring,)),
            dma((2, PLANE)),
            dma((units,)),
            dma((n_freq - 1,)),
            dma((n_freq - 1,)),
        ],
        compiler_params=pltpu.CompilerParams(
            collective_id=0, has_side_effects=True, vmem_limit_bytes=56 * 1024 * 1024
        ),
        name="forward",
    )(direction, green_blocks, block_mask.T, noise_weights, freq_index)

    chunks = 5
    return pl.pallas_call(
        back_kernel,
        out_shape=jax.ShapeDtypeStruct(direction.shape, BF16),
        in_specs=[anywhere] * 4,
        out_specs=anywhere,
        scratch_shapes=[
            vmem((keys, columns), BF16),
            vmem((1, columns), F32),
            vmem(direction.shape, BF16),
            vmem(direction.shape, BF16),
            pltpu.SMEM((NF,), jnp.int32),
            dma((3,)),
            dma((chunks,)),
            dma((chunks,)),
        ],
        compiler_params=pltpu.CompilerParams(vmem_limit_bytes=56 * 1024 * 1024),
        name="backward",
    )(images.reshape(keys, columns), prior_precision.reshape(1, columns), direction, freq_index)


def solution(mesh):
    n_freq = mesh.shape["freq"]
    ring = mesh.shape["param"] // PLANE
    placed = (
        P("freq", None, "param"),
        P("freq", None, None, "param"),
        P(None, "param"),
        P("freq", None),
        P("param"),
        P(),
    )
    return jax.shard_map(
        functools.partial(on_device, ring, n_freq),
        mesh=mesh,
        in_specs=placed,
        out_specs=P("freq", None, "param"),
        check_vma=False,
    )
```

time: 50.2 us -> 42.8 us (0.85)
  local copies, waits for them, and re-layouts: 4.89 us -> 0 us
  Pallas kernels: 45 us -> 42.7 us
    unnamed x12 -> x0, local copies, waits for them, and re-layouts: 4.89 us -> none
    pallas_call x1, Pallas kernels: 43.1 us -> 39.6 us  [on_device(): pl.pallas_call(functools.partial(forward_kernel, ring, n_freq), out_shape...]
    pallas_call x1, Pallas kernels: 1.89 us -> 3.06 us  [on_device(): pl.pallas_call(back_kernel, out_shape=jax.ShapeDtypeStruct(direction.shap...]
where the time goes in v2:
time: 42.8 us; the launch traced here: 42.7 us
  Pallas kernels  42.7 us (100%)
    pallas_call x1, Pallas kernels, on_device(): pl.pallas_call(functools.partial(forward_kernel, ring, n_freq), out_shape...  39.6 us
    pallas_call x1, Pallas kernels, on_device(): pl.pallas_call(back_kernel, out_shape=jax.ShapeDtypeStruct(direction.shap...  3.06 us

profile of v2, /device:TPU:1, one launch (start us, length us, event | category | flops | bytes accessed | tf_op | source)
XLA Modules:
  0.0 42.7 jit_solution(6938286025452909596)
XLA Ops:
  0.0 39.6 %forward.1 = bf16[4,32,512]{2,1,0:T(8,128)(2,1)} custom-call(bf16[105,8,512]{2,1,0:T(8,128)(2,1)} %dir_hbm.3, bf16[2,2,600,512]{3,2,1,0:T(8,128)(2,1)} %green_hbm.1, s32[4,8]{1,0:T(4,128)} %bitcast.4, f32[2,600]{1,0:T(2,128)} %noise_hbm.1, s32[8]{0:T(128)} %freq_hbm.3), custom_call_target="tpu_custom_call" | custom-call | tf_op jit(solution)/shard_map/forward/pallas_call | solution.py:357
  39.6 3.1 %backward.1 = bf16[105,8,512]{2,1,0:T(8,128)(2,1)} custom-call(bf16[128,512]{1,0:T(8,128)(2,1)} %bitcast.3, f32[1,512]{1,0:T(1,128)} %bitcast.5, bf16[105,8,512]{2,1,0:T(8,128)(2,1)} %dir_hbm.3, s32[8]{0:T(128)} %freq_hbm.3), custom_call_target="tpu_custom_call" | custom-call | tf_op jit(solution)/shard_map/backward/pallas_call | solution.py:404

commit v3 on v2

v3 whole, which is shorter than its diff:
```python
import functools
import math

import jax
import jax.numpy as jnp
from jax import lax
from jax.experimental import pallas as pl
from jax.experimental.pallas import tpu as pltpu
from jax.sharding import PartitionSpec as P

NT = 420
NF = 8
RHS = 8
SENSORS = 600
SBLK = 8
PBLK = 128
LANES = 128
PLANE = 8
ROW = 4
MESH = pl.DeviceIdType.MESH
F32 = jnp.float32
BF16 = jnp.bfloat16


def trig(freq, component, time):
    turn = freq * time + component * (NT // 4)
    phase = turn - NT * jnp.floor(turn * (1.0 / NT))
    phase = jnp.where(phase < 0, phase + NT, phase)
    phase = jnp.where(phase >= NT, phase - NT, phase)
    y = (jnp.abs(phase - NT // 2) - NT // 4) * (2.0 * math.pi / NT)
    s = y * y
    poly = -1.0 / 39916800
    for coef in (1.0 / 362880, -1.0 / 5040, 1.0 / 120, -1.0 / 6, 1.0):
        poly = poly * s + coef
    return poly * y * (1.0 / math.sqrt(NT))


def expanded_table(freq_ref, first_time, rows, columns, key_axis):
    key_shape = (rows, 1) if key_axis == 0 else (1, columns)
    step_shape = (1, columns) if key_axis == 0 else (rows, 1)
    key = lax.broadcasted_iota(jnp.int32, key_shape, key_axis)
    step = lax.broadcasted_iota(jnp.int32, step_shape, 1 - key_axis)
    freq = jnp.zeros(key_shape, F32)
    for w in range(NF):
        freq = jnp.where(key // (2 * RHS) == w, freq_ref[w].astype(F32), freq)
    component = (key // RHS % 2).astype(F32)
    time = (step // RHS + first_time).astype(F32)
    values = trig(freq, component, time)
    return jnp.where(key % RHS == step % RHS, values, 0.0)


def forward_kernel(
    ring, n_freq, dir_hbm, green_hbm, mask_hbm, noise_hbm, freq_hbm, prior_hbm,
    out_ref,
    dirs, green, mask_ref, noise_ref, freq_ref, prior_ref, kern, turned, mask, noise,
    spec_own, spec_send, spec_recv, data_send, data_recv, sum_send, sum_recv, weighted, image_send, images, back, damped,
    load_sem, dir_sem, near_sem,
    spec_ssem, spec_rsem, data_ssem, data_rsem, sum_ssem, sum_rsem, w_ssem, w_rsem, im_ssem, im_rsem,
):
    param = lax.axis_index("param")
    q = lax.axis_index("freq")
    k, z = param // ring, param % ring
    core = q % 2
    times = dirs.shape[0]
    columns = dirs.shape[2]
    own_w = NF // n_freq
    pair = 2 * RHS
    rows = own_w * pair
    tiles = -(-SENSORS // LANES)
    units = own_w * tiles
    padded = tiles * LANES
    extra = units - PLANE
    has_extra = k // extra == core

    def place(u):
        return (u, 0) if u < PLANE else (extra * core + u - PLANE, 1)

    def freq_peer(off):
        return (param, (q + off) % n_freq)

    def plane_peer(to):
        return (to * ring + z, q)

    def ring_peer(off):
        return (k * ring + (z + off) % ring, q)

    def remote(src, dst, ssem, rsem, to):
        return pltpu.make_async_remote_copy(
            src_ref=src, dst_ref=dst, send_sem=ssem, recv_sem=rsem, device_id=to, device_id_type=MESH
        )

    def signal(semaphore, to):
        pl.semaphore_signal(semaphore, inc=1, device_id=to, device_id_type=MESH)

    load_freq, load_mask, load_noise, load_prior, load_green = [
        pltpu.make_async_copy(src, dst, load_sem.at[i])
        for i, (src, dst) in enumerate(
            (
                (freq_hbm, freq_ref), (mask_hbm, mask_ref), (noise_hbm, noise_ref), (prior_hbm, prior_ref),
                (green_hbm, green),
            )
        )
    ]
    chunks = dir_sem.shape[0]
    size = times // chunks
    load_dirs = [
        pltpu.make_async_copy(dir_hbm.at[pl.ds(i * size, size)], dirs.at[pl.ds(i * size, size)], dir_sem.at[i])
        for i in range(chunks)
    ]
    for load in [load_freq] + load_dirs:
        load.start()

    y, x = k // ROW, k % ROW
    beside = [plane_peer(y * ROW + (x + 1) % ROW), plane_peer(y * ROW + (x + ROW - 1) % ROW)]
    across = [plane_peer((y + 1) % (PLANE // ROW) * ROW + x)]

    def along(d):
        return [ring_peer(d), ring_peer(ring - d)]

    barrier = pltpu.get_barrier_semaphore()
    peers = [freq_peer(o) for o in range(1, n_freq)] + beside + across + along(1)
    for peer in peers:
        signal(barrier, peer)
    rounds = [beside + across + along(1), beside + along(2), along(4)]

    def tell(i):
        for peer in rounds[i]:
            signal(near_sem.at[i], peer)

    def hear(i):
        pl.semaphore_wait(near_sem.at[i], len(rounds[i]))

    load_freq.wait()
    tables = [
        expanded_table(freq_ref, q * times + i * size, NF * pair, size * RHS, 0).astype(BF16) for i in range(chunks)
    ]
    part = jnp.zeros((NF * pair, columns), F32)
    for i in range(chunks):
        load_dirs[i].wait()
        steps = dirs[i * size : (i + 1) * size].astype(F32).reshape(size * RHS, columns).astype(BF16)
        part = part + jnp.dot(tables[i], steps, preferred_element_type=F32)
    for load in (load_mask, load_noise, load_green, load_prior):
        load.start()
    for g in range(n_freq):
        piece = part[g * rows : (g + 1) * rows]
        spec_own[g] = piece
        spec_send[g] = piece.astype(BF16)

    pl.semaphore_wait(barrier, len(peers))
    spec_copies = []
    for off in (2, 3, 1) if n_freq == 4 else range(1, n_freq):
        copy = remote(
            spec_send.at[(q + off) % n_freq], spec_recv.at[off - 1], spec_ssem.at[off - 1], spec_rsem.at[off - 1],
            freq_peer(off),
        )
        copy.start()
        spec_copies.append(copy)
    tell(0)

    load_mask.wait()
    sensor = lax.broadcasted_iota(jnp.int32, (padded, SBLK), 0)
    block = lax.broadcasted_iota(jnp.int32, (padded, SBLK), 1)
    per = SENSORS // SBLK
    picks = jnp.where((sensor >= block * per) & (sensor < (block + 1) * per), 1.0, 0.0).astype(BF16)
    block8 = lax.broadcasted_iota(jnp.int32, (SBLK, LANES), 0)
    parts = []
    for b in range(columns // PBLK):
        value = jnp.zeros((SBLK, LANES), F32)
        for s in range(SBLK):
            value = jnp.where(block8 == s, mask_ref[b, s].astype(F32), value)
        parts.append(value)
    blocks = jnp.concatenate(parts, axis=1).astype(BF16)
    mask[...] = jnp.dot(picks, blocks, preferred_element_type=F32).astype(BF16)
    load_green.wait()
    for w in range(own_w):
        for c in range(2):
            kern[w, c, :SENSORS, :] = green[w, c] * mask[:SENSORS, :]
            kern[w, c, SENSORS:, :] = jnp.zeros((padded - SENSORS, columns), BF16)
    hear(0)
    tell(1)
    for w in range(own_w):
        for c in range(2):
            turned[w, c] = kern[w, c].T
    load_noise.wait()
    noise[...] = jnp.zeros_like(noise)
    for u in range(units):
        w, j = u // tiles, u % tiles
        width = min(LANES, SENSORS - j * LANES)
        row, half = place(u)
        noise[row, half, :, :width] = jnp.broadcast_to(
            noise_ref[w : w + 1, j * LANES : j * LANES + width], (pair, width)
        )
    hear(1)
    tell(2)

    total = spec_own[q]
    for off, copy in zip((2, 3, 1) if n_freq == 4 else range(1, n_freq), spec_copies):
        copy.wait_recv()
        total = total + spec_recv[off - 1].astype(F32)

    for w in range(own_w):
        first = total[w * pair : (w + 1) * pair]
        second = jnp.concatenate([-first[RHS:], first[:RHS]], axis=0)
        data = jnp.dot(first.astype(BF16), turned[w, 0], preferred_element_type=F32) + jnp.dot(
            second.astype(BF16), turned[w, 1], preferred_element_type=F32
        )
        data = data.astype(BF16)
        for j in range(tiles):
            row, half = place(w * tiles + j)
            data_send[row, half] = data[:, j * LANES : (j + 1) * LANES]

    def data_copy(off, count):
        to, here = (k + off) % PLANE, pl.ds(0, count)
        return remote(
            data_send.at[to, here], data_recv.at[off, here], data_ssem.at[off], data_rsem.at[off], plane_peer(to)
        )

    def sum_copy(off, count):
        here = pl.ds(0, count)
        return remote(sum_send.at[here], sum_recv.at[off, here], sum_ssem.at[off], sum_rsem.at[off], ring_peer(off))

    def weighted_copy(off, count):
        own = weighted.at[k, pl.ds(0, count)]
        return remote(own, own, w_ssem.at[off], w_rsem.at[k], plane_peer((k + off) % PLANE))

    def weighted_arrival(owner, count):
        own = weighted.at[owner, pl.ds(0, count)]
        return remote(own, own, w_ssem.at[0], w_rsem.at[owner], plane_peer((k + 1) % PLANE))

    far_plane = [off for off in (6, 2, 5, 7, 3, 1, 4)]
    far_ring = sorted(range(1, ring), key=lambda off: -min(off, ring - off))

    for off in far_plane:
        two = (k + off) % PLANE // extra == core
        pl.when(two)(data_copy(off, 2).start)
        pl.when(jnp.logical_not(two))(data_copy(off, 1).start)

    for i in range(chunks):
        first_time = q * times + i * size
        back[i] = (2.0 * expanded_table(freq_ref, first_time, size * RHS, NF * pair, 1)).astype(BF16)
    load_prior.wait()
    for i in range(chunks):
        steps = dirs[i * size : (i + 1) * size].astype(F32).reshape(size * RHS, columns)
        damped[i] = steps * prior_ref[...]

    def reduce(count):
        acc = data_send[k, :count].astype(F32)
        for off in reversed(far_plane):
            data_copy(off, count).wait_recv()
            acc = acc + data_recv[off, :count].astype(F32)
        sum_send[:count] = acc.astype(BF16)
        hear(2)
        for off in far_ring:
            sum_copy(off, count).start()
        for off in reversed(far_ring):
            sum_copy(off, count).wait_recv()
            acc = acc + sum_recv[off, :count].astype(F32)
        weighted[k, :count] = (acc * noise[k, :count]).astype(BF16)
        for off in far_plane:
            weighted_copy(off, count).start()

    def finish(count):
        for off in far_ring:
            sum_copy(off, count).wait_send()
        for off in far_plane:
            weighted_copy(off, count).wait_send()

    pl.when(has_extra)(functools.partial(reduce, 2))
    pl.when(jnp.logical_not(has_extra))(functools.partial(reduce, 1))

    for owner in range(PLANE):
        two = owner // extra == core
        other = k != owner
        pl.when(jnp.logical_and(other, two))(weighted_arrival(owner, 2).wait_recv)
        pl.when(jnp.logical_and(other, jnp.logical_not(two)))(weighted_arrival(owner, 1).wait_recv)

    image_copies = []
    for w in range(own_w):
        here = slice(w * pair, (w + 1) * pair)
        first = jnp.concatenate([weighted[place(w * tiles + j)] for j in range(tiles)], axis=1)
        wide = first.astype(F32)
        second = jnp.concatenate([wide[RHS:], -wide[:RHS]], axis=0).astype(BF16)
        image = jnp.dot(first, kern[w, 0], preferred_element_type=F32) + jnp.dot(
            second, kern[w, 1], preferred_element_type=F32
        )
        image = image.astype(BF16)
        image_send[w] = image
        images[q, w] = image
        for off in (2, 3, 1) if n_freq == 4 else range(1, n_freq):
            copy = remote(
                image_send.at[w], images.at[q, w], im_ssem.at[w, off - 1], im_rsem.at[w, off - 1], freq_peer(off)
            )
            copy.start()
            image_copies.append(copy)

    for copy in spec_copies:
        copy.wait_send()
    for off in far_plane:
        two = (k + off) % PLANE // extra == core
        pl.when(two)(data_copy(off, 2).wait_send)
        pl.when(jnp.logical_not(two))(data_copy(off, 1).wait_send)
    pl.when(has_extra)(functools.partial(finish, 2))
    pl.when(jnp.logical_not(has_extra))(functools.partial(finish, 1))
    for copy in image_copies:
        copy.wait_recv()
    every = images[...].reshape(NF * pair, columns)
    for i in range(chunks):
        summed = jnp.dot(back[i], every, preferred_element_type=F32)
        out_ref[i * size : (i + 1) * size] = (summed + damped[i]).reshape(size, RHS, columns).astype(BF16)
    for copy in image_copies:
        copy.wait_send()


def on_device(ring, n_freq, direction, green_blocks, block_mask, noise_weights, prior_precision, freq_index):
    times, _, columns = direction.shape
    own_w = NF // n_freq
    pair = 2 * RHS
    rows = own_w * pair
    keys = NF * pair
    tiles = -(-SENSORS // LANES)
    padded = tiles * LANES
    vmem = pltpu.VMEM
    dma = pltpu.SemaphoreType.DMA
    chunks = 3
    size = times // chunks
    operands = (
        direction, green_blocks, block_mask.T, noise_weights, freq_index, prior_precision.reshape(1, columns)
    )
    return pl.pallas_call(
        functools.partial(forward_kernel, ring, n_freq),
        out_shape=vmem(direction.shape, BF16),
        in_specs=[pl.BlockSpec(memory_space=pltpu.HBM)] * len(operands),
        out_specs=pl.BlockSpec(memory_space=vmem),
        scratch_shapes=[
            vmem((times, RHS, columns), BF16),
            vmem((own_w, 2, SENSORS, columns), BF16),
            pltpu.SMEM(block_mask.shape[::-1], jnp.int32),
            vmem((own_w, SENSORS), F32),
            pltpu.SMEM((NF,), jnp.int32),
            vmem((1, columns), F32),
            vmem((own_w, 2, padded, columns), BF16),
            vmem((own_w, 2, columns, padded), BF16),
            vmem((padded, columns), BF16),
            vmem((PLANE, 2, pair, LANES), F32),
            vmem((n_freq, rows, columns), F32),
            vmem((n_freq, rows, columns), BF16),
            vmem((n_freq - 1, rows, columns), BF16),
            vmem((PLANE, 2, pair, LANES), BF16),
            vmem((PLANE, 2, pair, LANES), BF16),
            vmem((2, pair, LANES), BF16),
            vmem((ring, 2, pair, LANES), BF16),
            vmem((PLANE, 2, pair, LANES), BF16),
            vmem((own_w, pair, columns), BF16),
            vmem((n_freq, own_w, pair, columns), BF16),
            vmem((chunks, size * RHS, keys), BF16),
            vmem((chunks, size * RHS, columns), F32),
            dma((5,)),
            dma((chunks,)),
            pltpu.SemaphoreType.REGULAR((3,)),
            dma((n_freq - 1,)),
            dma((n_freq - 1,)),
            dma((PLANE,)),
            dma((PLANE,)),
            dma((ring,)),
            dma((ring,)),
            dma((PLANE,)),
            dma((PLANE,)),
            dma((own_w, n_freq - 1)),
            dma((own_w, n_freq - 1)),
        ],
        compiler_params=pltpu.CompilerParams(
            collective_id=0, has_side_effects=True, vmem_limit_bytes=40 * 1024 * 1024
        ),
        name="forward",
    )(*(pltpu.with_memory_space_constraint(operand, pltpu.HBM) for operand in operands))


def solution(mesh):
    n_freq = mesh.shape["freq"]
    ring = mesh.shape["param"] // PLANE
    placed = (
        P("freq", None, "param"),
        P("freq", None, None, "param"),
        P(None, "param"),
        P("freq", None),
        P("param"),
        P(),
    )
    return jax.shard_map(
        functools.partial(on_device, ring, n_freq),
        mesh=mesh,
        in_specs=placed,
        out_specs=P("freq", None, "param"),
        check_vma=False,
    )
```

time: 42.8 us -> 40.4 us (0.944)
  Pallas kernels: 42.7 us -> 39.4 us
  local copies, waits for them, and re-layouts: 0 us -> 0.91 us
    pallas_call x1 -> x0, Pallas kernels: 3.06 us -> none  [on_device(): pl.pallas_call(back_kernel, out_shape=jax.ShapeDtypeStruct(direction.shap...]
    unnamed x0 -> x1, local copies, waits for them, and re-layouts: none -> 0.91 us
where the time goes in v3:
time: 40.4 us; the launch traced here: 40.3 us
  Pallas kernels  39.4 us (98%)
  local copies, waits for them, and re-layouts  0.91 us (2%)
    pallas_call x1, Pallas kernels, on_device(): pl.pallas_call(functools.partial(forward_kernel, ring, n_freq), out_shape...  39.4 us
    unnamed x1, local copies, waits for them, and re-layouts  0.91 us

profile of v3, /device:TPU:1, one launch (start us, length us, event | category | flops | bytes accessed | tf_op | source)
XLA Modules:
  0.0 40.3 jit_solution(14039737214002197323)
XLA Ops:
  0.0 39.4 %forward.1 = bf16[105,8,512]{2,1,0:T(8,128)(2,1)S(1)} custom-call(bf16[105,8,512]{2,1,0:T(8,128)(2,1)} %dir_hbm.1, bf16[2,2,600,512]{3,2,1,0:T(8,128)(2,1)} %green_hbm.1, s32[4,8]{1,0:T(4,128)} %bitcast.2, f32[2,600]{1,0:T(2,128)} %noise_hbm.1, s32[8]{0:T(128)} %freq_hbm.1, f32[1,512]{1,0:T(1,128)} %bitcast.3), custom_call_target="tpu_custom_call" | custom-call | tf_op jit(solution)/shard_map/forward/pallas_call | solution.py:329
  39.4 0.9 %copy.8 = bf16[105,8,512]{2,1,0:T(8,128)(2,1)} copy(bf16[105,8,512]{2,1,0:T(8,128)(2,1)S(1)} %forward.1) | data formatting | bytes 1720320

commit v4 on v3

--- a/solution.py
+++ b/solution.py
@@ -69,11 +69,11 @@
     tiles = -(-SENSORS // LANES)
     units = own_w * tiles
     padded = tiles * LANES
-    extra = units - PLANE
+    extra = 2 * (units - PLANE)
     has_extra = k // extra == core
 
-    def place(u):
-        return (u, 0) if u < PLANE else (extra * core + u - PLANE, 1)
+    def place(u, half):
+        return (u, half) if u < PLANE else (extra * core + 2 * (u - PLANE) + half, 2)
 
     def freq_peer(off):
         return (param, (q + off) % n_freq)
@@ -130,9 +130,20 @@
     def hear(i):
         pl.semaphore_wait(near_sem.at[i], len(rounds[i]))
 
+    key = lax.broadcasted_iota(jnp.int32, (NF * pair, 1), 0)
+    step = lax.broadcasted_iota(jnp.int32, (1, LANES), 1)
+    row = lax.broadcasted_iota(jnp.int32, (NF * pair, size * RHS), 0)
+    column = lax.broadcasted_iota(jnp.int32, (NF * pair, size * RHS), 1)
+    same_side = row % RHS == column % RHS
+    repeats = [jnp.where(row == column // RHS + i * size, 1.0, 0.0).astype(BF16) for i in range(chunks)]
     load_freq.wait()
+    freq = jnp.zeros(key.shape, F32)
+    for w in range(NF):
+        freq = jnp.where(key // pair == w, freq_ref[w].astype(F32), freq)
+    narrow = trig(freq, (key // RHS % 2).astype(F32), (step + q * times).astype(F32)).astype(BF16)
     tables = [
-        expanded_table(freq_ref, q * times + i * size, NF * pair, size * RHS, 0).astype(BF16) for i in range(chunks)
+        jnp.where(same_side, jnp.dot(narrow, repeat, preferred_element_type=F32), 0.0).astype(BF16)
+        for repeat in repeats
     ]
     part = jnp.zeros((NF * pair, columns), F32)
     for i in range(chunks):
@@ -186,10 +197,11 @@
     for u in range(units):
         w, j = u // tiles, u % tiles
         width = min(LANES, SENSORS - j * LANES)
-        row, half = place(u)
-        noise[row, half, :, :width] = jnp.broadcast_to(
-            noise_ref[w : w + 1, j * LANES : j * LANES + width], (pair, width)
-        )
+        for half in range(2):
+            row, part = place(u, half)
+            noise[row, part, :, :width] = jnp.broadcast_to(
+                noise_ref[w : w + 1, j * LANES : j * LANES + width], (RHS, width)
+            )
     hear(1)
     tell(2)
 
@@ -204,10 +216,10 @@
         data = jnp.dot(first.astype(BF16), turned[w, 0], preferred_element_type=F32) + jnp.dot(
             second.astype(BF16), turned[w, 1], preferred_element_type=F32
         )
-        data = data.astype(BF16)
         for j in range(tiles):
-            row, half = place(w * tiles + j)
-            data_send[row, half] = data[:, j * LANES : (j + 1) * LANES]
+            for half in range(2):
+                row, part = place(w * tiles + j, half)
+                data_send[row, part] = data[half * RHS : (half + 1) * RHS, j * LANES : (j + 1) * LANES].astype(BF16)
 
     def data_copy(off, count):
         to, here = (k + off) % PLANE, pl.ds(0, count)
@@ -232,8 +244,8 @@
 
     for off in far_plane:
         two = (k + off) % PLANE // extra == core
-        pl.when(two)(data_copy(off, 2).start)
-        pl.when(jnp.logical_not(two))(data_copy(off, 1).start)
+        pl.when(two)(data_copy(off, 3).start)
+        pl.when(jnp.logical_not(two))(data_copy(off, 2).start)
 
     for i in range(chunks):
         first_time = q * times + i * size
@@ -265,21 +277,23 @@
         for off in far_plane:
             weighted_copy(off, count).wait_send()
 
-    pl.when(has_extra)(functools.partial(reduce, 2))
-    pl.when(jnp.logical_not(has_extra))(functools.partial(reduce, 1))
-
-    for owner in range(PLANE):
-        two = owner // extra == core
-        other = k != owner
-        pl.when(jnp.logical_and(other, two))(weighted_arrival(owner, 2).wait_recv)
-        pl.when(jnp.logical_and(other, jnp.logical_not(two)))(weighted_arrival(owner, 1).wait_recv)
+    pl.when(has_extra)(functools.partial(reduce, 3))
+    pl.when(jnp.logical_not(has_extra))(functools.partial(reduce, 2))
 
     image_copies = []
     for w in range(own_w):
-        here = slice(w * pair, (w + 1) * pair)
-        first = jnp.concatenate([weighted[place(w * tiles + j)] for j in range(tiles)], axis=1)
-        wide = first.astype(F32)
-        second = jnp.concatenate([wide[RHS:], -wide[:RHS]], axis=0).astype(BF16)
+        for owner in range(PLANE) if w == 0 else ():
+            two = owner // extra == core
+            other = k != owner
+            pl.when(jnp.logical_and(other, two))(weighted_arrival(owner, 3).wait_recv)
+            pl.when(jnp.logical_and(other, jnp.logical_not(two)))(weighted_arrival(owner, 2).wait_recv)
+        halves = [
+            jnp.concatenate([weighted[place(w * tiles + j, half)].astype(F32) for j in range(tiles)], axis=1)
+            for half in range(2)
+        ]
+        wide = jnp.concatenate(halves, axis=0)
+        first = wide.astype(BF16)
+        second = jnp.concatenate([halves[1], -halves[0]], axis=0).astype(BF16)
         image = jnp.dot(first, kern[w, 0], preferred_element_type=F32) + jnp.dot(
             second, kern[w, 1], preferred_element_type=F32
         )
@@ -297,10 +311,10 @@
         copy.wait_send()
     for off in far_plane:
         two = (k + off) % PLANE // extra == core
-        pl.when(two)(data_copy(off, 2).wait_send)
-        pl.when(jnp.logical_not(two))(data_copy(off, 1).wait_send)
-    pl.when(has_extra)(functools.partial(finish, 2))
-    pl.when(jnp.logical_not(has_extra))(functools.partial(finish, 1))
+        pl.when(two)(data_copy(off, 3).wait_send)
+        pl.when(jnp.logical_not(two))(data_copy(off, 2).wait_send)
+    pl.when(has_extra)(functools.partial(finish, 3))
+    pl.when(jnp.logical_not(has_extra))(functools.partial(finish, 2))
     for copy in image_copies:
         copy.wait_recv()
     every = images[...].reshape(NF * pair, columns)
@@ -341,15 +355,15 @@
             vmem((own_w, 2, padded, columns), BF16),
             vmem((own_w, 2, columns, padded), BF16),
             vmem((padded, columns), BF16),
-            vmem((PLANE, 2, pair, LANES), F32),
+            vmem((PLANE, 3, RHS, LANES), F32),
             vmem((n_freq, rows, columns), F32),
             vmem((n_freq, rows, columns), BF16),
             vmem((n_freq - 1, rows, columns), BF16),
-            vmem((PLANE, 2, pair, LANES), BF16),
-            vmem((PLANE, 2, pair, LANES), BF16),
-            vmem((2, pair, LANES), BF16),
-            vmem((ring, 2, pair, LANES), BF16),
-            vmem((PLANE, 2, pair, LANES), BF16),
+            vmem((PLANE, 3, RHS, LANES), BF16),
+            vmem((PLANE, 3, RHS, LANES), BF16),
+            vmem((3, RHS, LANES), BF16),
+            vmem((ring, 3, RHS, LANES), BF16),
+            vmem((PLANE, 3, RHS, LANES), BF16),
             vmem((own_w, pair, columns), BF16),
             vmem((n_freq, own_w, pair, columns), BF16),
             vmem((chunks, size * RHS, keys), BF16),

time: 40.4 us -> 39.7 us (0.983)
  Pallas kernels: 39.4 us -> 38.6 us
    pallas_call x1, Pallas kernels: 39.4 us -> 38.6 us  [on_device(): pl.pallas_call(functools.partial(forward_kernel, ring, n_freq), out_shape...]
where the time goes in v4:
time: 39.7 us; the launch traced here: 39.6 us
  Pallas kernels  38.6 us (97%)
  local copies, waits for them, and re-layouts  0.91 us (2%)
    pallas_call x1, Pallas kernels, on_device(): pl.pallas_call(functools.partial(forward_kernel, ring, n_freq), out_shape...  38.6 us
    unnamed x1, local copies, waits for them, and re-layouts  0.91 us

profile of v4, /device:TPU:1, one launch (start us, length us, event | category | flops | bytes accessed | tf_op | source)
XLA Modules:
  0.0 39.6 jit_solution(12229268325474389774)
XLA Ops:
  0.0 38.6 %forward.1 = bf16[105,8,512]{2,1,0:T(8,128)(2,1)S(1)} custom-call(bf16[105,8,512]{2,1,0:T(8,128)(2,1)} %dir_hbm.1, bf16[2,2,600,512]{3,2,1,0:T(8,128)(2,1)} %green_hbm.1, s32[4,8]{1,0:T(4,128)} %bitcast.2, f32[2,600]{1,0:T(2,128)} %noise_hbm.1, s32[8]{0:T(128)} %freq_hbm.1, f32[1,512]{1,0:T(1,128)} %bitcast.3), custom_call_target="tpu_custom_call" | custom-call | tf_op jit(solution)/shard_map/forward/pallas_call | solution.py:343
  38.7 0.9 %copy.8 = bf16[105,8,512]{2,1,0:T(8,128)(2,1)} copy(bf16[105,8,512]{2,1,0:T(8,128)(2,1)S(1)} %forward.1) | data formatting | bytes 1720320

commit v5 on v4

--- a/solution.py
+++ b/solution.py
@@ -154,7 +154,6 @@
         load.start()
     for g in range(n_freq):
         piece = part[g * rows : (g + 1) * rows]
-        spec_own[g] = piece
         spec_send[g] = piece.astype(BF16)
 
     pl.semaphore_wait(barrier, len(peers))
@@ -167,6 +166,8 @@
         copy.start()
         spec_copies.append(copy)
     tell(0)
+    for g in range(n_freq):
+        spec_own[g] = part[g * rows : (g + 1) * rows]
 
     load_mask.wait()
     sensor = lax.broadcasted_iota(jnp.int32, (padded, SBLK), 0)
@@ -182,13 +183,13 @@
         parts.append(value)
     blocks = jnp.concatenate(parts, axis=1).astype(BF16)
     mask[...] = jnp.dot(picks, blocks, preferred_element_type=F32).astype(BF16)
+    hear(0)
+    tell(1)
     load_green.wait()
     for w in range(own_w):
         for c in range(2):
             kern[w, c, :SENSORS, :] = green[w, c] * mask[:SENSORS, :]
             kern[w, c, SENSORS:, :] = jnp.zeros((padded - SENSORS, columns), BF16)
-    hear(0)
-    tell(1)
     for w in range(own_w):
         for c in range(2):
             turned[w, c] = kern[w, c].T

time: 39.7 us -> 39.9 us (level)
  no operation moved by 1% of the time
where the time goes in v5:
time: 39.9 us; the launch traced here: 39.8 us
  Pallas kernels  38.9 us (97%)
  local copies, waits for them, and re-layouts  0.91 us (2%)
    pallas_call x1, Pallas kernels, on_device(): pl.pallas_call(functools.partial(forward_kernel, ring, n_freq), out_shape...  38.9 us
    unnamed x1, local copies, waits for them, and re-layouts  0.91 us

profile of v5, /device:TPU:1, one launch (start us, length us, event | category | flops | bytes accessed | tf_op | source)
XLA Modules:
  0.0 39.8 jit_solution(1579531054032877916)
XLA Ops:
  0.0 38.9 %forward.1 = bf16[105,8,512]{2,1,0:T(8,128)(2,1)S(1)} custom-call(bf16[105,8,512]{2,1,0:T(8,128)(2,1)} %dir_hbm.1, bf16[2,2,600,512]{3,2,1,0:T(8,128)(2,1)} %green_hbm.1, s32[4,8]{1,0:T(4,128)} %bitcast.2, f32[2,600]{1,0:T(2,128)} %noise_hbm.1, s32[8]{0:T(128)} %freq_hbm.1, f32[1,512]{1,0:T(1,128)} %bitcast.3), custom_call_target="tpu_custom_call" | custom-call | tf_op jit(solution)/shard_map/forward/pallas_call | solution.py:344
  38.9 0.9 %copy.8 = bf16[105,8,512]{2,1,0:T(8,128)(2,1)} copy(bf16[105,8,512]{2,1,0:T(8,128)(2,1)S(1)} %forward.1) | data formatting | bytes 1720320

commit v6 on v4

--- a/solution.py
+++ b/solution.py
@@ -153,19 +153,23 @@
     for load in (load_mask, load_noise, load_green, load_prior):
         load.start()
     for g in range(n_freq):
-        piece = part[g * rows : (g + 1) * rows]
-        spec_own[g] = piece
-        spec_send[g] = piece.astype(BF16)
+        for w in range(own_w):
+            piece = part[g * rows + w * pair : g * rows + (w + 1) * pair]
+            spec_own[g, w] = piece
+            spec_send[g, w] = piece.astype(BF16)
 
     pl.semaphore_wait(barrier, len(peers))
-    spec_copies = []
-    for off in (2, 3, 1) if n_freq == 4 else range(1, n_freq):
-        copy = remote(
-            spec_send.at[(q + off) % n_freq], spec_recv.at[off - 1], spec_ssem.at[off - 1], spec_rsem.at[off - 1],
-            freq_peer(off),
-        )
-        copy.start()
-        spec_copies.append(copy)
+    far_freq = (2, 3, 1) if n_freq == 4 else tuple(range(1, n_freq))
+
+    def spec_copy(w, off):
+        return remote(
+            spec_send.at[(q + off) % n_freq, w], spec_recv.at[off - 1, w],
+            spec_ssem.at[w, off - 1], spec_rsem.at[w, off - 1], freq_peer(off),
+        )
+
+    for w in range(own_w):
+        for off in far_freq:
+            spec_copy(w, off).start()
     tell(0)
 
     load_mask.wait()
@@ -205,13 +209,11 @@
     hear(1)
     tell(2)
 
-    total = spec_own[q]
-    for off, copy in zip((2, 3, 1) if n_freq == 4 else range(1, n_freq), spec_copies):
-        copy.wait_recv()
-        total = total + spec_recv[off - 1].astype(F32)
-
-    for w in range(own_w):
-        first = total[w * pair : (w + 1) * pair]
+    for w in range(own_w):
+        first = spec_own[q, w]
+        for off in far_freq:
+            spec_copy(w, off).wait_recv()
+            first = first + spec_recv[off - 1, w].astype(F32)
         second = jnp.concatenate([-first[RHS:], first[:RHS]], axis=0)
         data = jnp.dot(first.astype(BF16), turned[w, 0], preferred_element_type=F32) + jnp.dot(
             second.astype(BF16), turned[w, 1], preferred_element_type=F32
@@ -307,8 +309,9 @@
             copy.start()
             image_copies.append(copy)
 
-    for copy in spec_copies:
-        copy.wait_send()
+    for w in range(own_w):
+        for off in far_freq:
+            spec_copy(w, off).wait_send()
     for off in far_plane:
         two = (k + off) % PLANE // extra == core
         pl.when(two)(data_copy(off, 3).wait_send)
@@ -356,9 +359,9 @@
             vmem((own_w, 2, columns, padded), BF16),
             vmem((padded, columns), BF16),
             vmem((PLANE, 3, RHS, LANES), F32),
-            vmem((n_freq, rows, columns), F32),
-            vmem((n_freq, rows, columns), BF16),
-            vmem((n_freq - 1, rows, columns), BF16),
+            vmem((n_freq, own_w, pair, columns), F32),
+            vmem((n_freq, own_w, pair, columns), BF16),
+            vmem((n_freq - 1, own_w, pair, columns), BF16),
             vmem((PLANE, 3, RHS, LANES), BF16),
             vmem((PLANE, 3, RHS, LANES), BF16),
             vmem((3, RHS, LANES), BF16),
@@ -371,8 +374,8 @@
             dma((5,)),
             dma((chunks,)),
             pltpu.SemaphoreType.REGULAR((3,)),
-            dma((n_freq - 1,)),
-            dma((n_freq - 1,)),
+            dma((own_w, n_freq - 1)),
+            dma((own_w, n_freq - 1)),
             dma((PLANE,)),
             dma((PLANE,)),
             dma((ring,)),

time: 39.7 us -> 39.9 us (level)
  no operation moved by 1% of the time
where the time goes in v6:
time: 39.9 us; the launch traced here: 39.7 us
  Pallas kernels  38.8 us (97%)
  local copies, waits for them, and re-layouts  0.91 us (2%)
    pallas_call x1, Pallas kernels, on_device(): pl.pallas_call(functools.partial(forward_kernel, ring, n_freq), out_shape...  38.8 us
    unnamed x1, local copies, waits for them, and re-layouts  0.91 us

profile of v6, /device:TPU:1, one launch (start us, length us, event | category | flops | bytes accessed | tf_op | source)
XLA Modules:
  0.0 39.7 jit_solution(5056720271215476505)
XLA Ops:
  0.0 38.8 %forward.1 = bf16[105,8,512]{2,1,0:T(8,128)(2,1)S(1)} custom-call(bf16[105,8,512]{2,1,0:T(8,128)(2,1)} %dir_hbm.1, bf16[2,2,600,512]{3,2,1,0:T(8,128)(2,1)} %green_hbm.1, s32[4,8]{1,0:T(4,128)} %bitcast.2, f32[2,600]{1,0:T(2,128)} %noise_hbm.1, s32[8]{0:T(128)} %freq_hbm.1, f32[1,512]{1,0:T(1,128)} %bitcast.3), custom_call_target="tpu_custom_call" | custom-call | tf_op jit(solution)/shard_map/forward/pallas_call | solution.py:346
  38.8 0.9 %copy.8 = bf16[105,8,512]{2,1,0:T(8,128)(2,1)} copy(bf16[105,8,512]{2,1,0:T(8,128)(2,1)S(1)} %forward.1) | data formatting | bytes 1720320
